TPU v7x, 32 devices: a whole 2x2x4 slice. The times are simulated.
32 devices in a mesh: grp: 8 (over z, y), row: 4 (over x, core).
Axes of the slice: x: 2, y: 2, z: 4, core: 2. Of those that a mesh axis runs over, the one named last changes fastest.
Arguments:
- grads: float32 [12, 4, 1792, 1024], P(None, 'row', 'grp'), may hold values from -320 to 320
- momentum: float32 [12, 4, 1792, 1024], P(None, 'row', 'grp'), may hold values from -640 to 640
- owner_table: int32 [12], replicated, may hold values from 0 to 8, as said below
Outputs:
- new_momentum: float32 [12, 4, 1792, 1024], P(None, 'row', 'grp')
- update: float32 [12, 4, 1792, 1024], P(None, 'row', 'grp')
Inputs may be any that keep to these rules, and one draw needn't show every extreme that they name: `owner_table`: each value 0 to 7 appears exactly once; the other entries equal 8.
All inputs are finite; a program needn't handle non-finite values.
Results may differ from a plain program's by a relative error of at most 0.0001.
Values sent between devices are 32-bit elements; how exact they have to be, the bound alone decides.
A program may use at most 128 MiB of HBM per device.

v0:
```python
import math

import jax
import jax.numpy as jnp
from jax import lax
from jax.experimental import pallas as pl
from jax.experimental.pallas import tpu as pltpu
from jax.sharding import Mesh
from jax.sharding import PartitionSpec as P

momentum_decay = 0.95
norm_epsilon = 1e-07
first_coef = 3.4445
second_coef = -4.775
third_coef = 2.0315

STRIPES = 4


def dot3(left, right, dims=(((1,), (0,)), ((), ()))):
    return lax.dot_general(
        left, right, dims, precision=lax.Precision.HIGH, preferred_element_type=jnp.float32
    )


def pick_kernel(chosen_ref, grads_ref, momentum_ref, out_ref):
    grad = grads_ref[0, 0]
    out_ref[0] = grad + momentum_decay * (momentum_decay * momentum_ref[0, 0] + grad)


def pick_nesterov(chosen, grads, momentum, groups):
    rows, width = grads.shape[2:]
    state = pl.BlockSpec((1, 1, rows, width), lambda g, chosen: (chosen[g], 0, 0, 0))
    return pl.pallas_call(
        pick_kernel,
        grid_spec=pltpu.PrefetchScalarGridSpec(
            num_scalar_prefetch=1,
            grid=(groups,),
            in_specs=[state, state],
            out_specs=pl.BlockSpec((1, rows, width), lambda g, chosen: (g, 0, 0)),
        ),
        out_shape=jax.ShapeDtypeStruct((groups, rows, width), jnp.float32),
        cost_estimate=pl.CostEstimate(
            flops=4 * groups * rows * width, bytes_accessed=12 * groups * rows * width, transcendentals=0
        ),
    )(chosen, grads, momentum)


def place_kernel(groups, owner_ref, returned_ref, out_ref):
    inside = owner_ref[pl.program_id(0)] < groups

    @pl.when(inside)
    def _():
        out_ref[0, 0] = returned_ref[0]

    @pl.when(jnp.logical_not(inside))
    def _():
        out_ref[...] = jnp.zeros_like(out_ref)


def place_update(owner_table, returned, mats):
    groups, rows, width = returned.shape

    def kernel(*refs):
        place_kernel(groups, *refs)

    return pl.pallas_call(
        kernel,
        grid_spec=pltpu.PrefetchScalarGridSpec(
            num_scalar_prefetch=1,
            grid=(mats,),
            in_specs=[
                pl.BlockSpec(
                    (1, rows, width), lambda k, owner: (jnp.minimum(owner[k], groups - 1), 0, 0)
                )
            ],
            out_specs=pl.BlockSpec((1, 1, rows, width), lambda k, owner: (k, 0, 0, 0)),
        ),
        out_shape=jax.ShapeDtypeStruct((mats, 1, rows, width), jnp.float32),
        cost_estimate=pl.CostEstimate(
            flops=0, bytes_accessed=4 * (groups + mats) * rows * width, transcendentals=0
        ),
    )(owner_table, returned)


def upper_gram(current):
    width = current.shape[1]
    size = width // STRIPES
    return jnp.concatenate(
        [
            dot3(
                current[:, i * size : (i + 1) * size],
                current[:, i * size :],
                (((0,), (0,)), ((), ())),
            )
            for i in range(STRIPES)
        ],
        axis=1,
    )


def triangle(packed):
    half = packed.shape[0] // 2
    parts, at = [], 0
    for i in range(STRIPES):
        end = at + (STRIPES - i) * 2 * half
        parts += [packed[:half, at:end], packed[half:, at + half : end]]
        at = end
    return jnp.concatenate(parts, axis=1)


def split(values):
    head = values.astype(jnp.bfloat16)
    return head, (values - head.astype(jnp.float32)).astype(jnp.bfloat16)


def product(left, right_head, right_tail):
    head, tail = split(left)
    whole = right_head[...]
    small = jnp.dot(head, right_tail[...], preferred_element_type=jnp.float32)
    small += jnp.dot(tail, whole, preferred_element_type=jnp.float32)
    return small + jnp.dot(head, whole, preferred_element_type=jnp.float32)


def polynomial_kernel(
    scale, packed_ref, head_ref, tail_ref, factor_ref, gram, gram_head, gram_tail, low, low_head, low_tail
):
    size = packed_ref.shape[0]
    width = gram.shape[0]
    count = width // size
    tile = min(256, width)

    total = jnp.zeros((size, size), jnp.float32)
    diagonal = lax.broadcasted_iota(jnp.int32, (size, size), 0) == lax.broadcasted_iota(
        jnp.int32, (size, size), 1
    )
    at = 0
    for i in range(count):
        total += jnp.where(diagonal, packed_ref[:, at : at + size], 0.0)
        at += (count - i) * size
    total = jnp.full((1, width), jnp.sum(total), jnp.float32)
    inverse = 1.0 / (jnp.sqrt(total) + norm_epsilon)
    square = inverse * inverse
    factor = inverse * scale
    factor_ref[...] = jnp.broadcast_to(first_coef * first_coef * factor, factor_ref.shape)

    at = 0
    for i in range(count):
        for j in range(i, count):
            block = packed_ref[:, at : at + size] * square[:, :size]
            at += size
            gram[i * size : (i + 1) * size, j * size : (j + 1) * size] = block
            if j > i:
                gram[j * size : (j + 1) * size, i * size : (i + 1) * size] = block.T

    @pl.loop(0, width // tile)
    def _(t):
        rows = pl.ds(pl.multiple_of(t * tile, tile), tile)
        gram_head[rows, :], gram_tail[rows, :] = split(gram[rows, :])

    @pl.loop(0, width // tile)
    def _(t):
        rows = pl.ds(pl.multiple_of(t * tile, tile), tile)
        own = gram[rows, :]
        values = second_coef * own + third_coef * product(own, gram_head, gram_tail)
        low[rows, :] = values
        low_head[rows, :], low_tail[rows, :] = split(values)

    @pl.loop(0, width // tile)
    def _(t):
        rows = pl.ds(pl.multiple_of(t * tile, tile), tile)
        own = gram[rows, :]
        own = first_coef * own + product(own, low_head, low_tail)
        own = first_coef * own + product(own, low_head, low_tail)
        gram[rows, :] = own
        gram_head[rows, :], gram_tail[rows, :] = split(own)

    @pl.loop(0, width // tile)
    def _(t):
        rows = pl.ds(pl.multiple_of(t * tile, tile), tile)
        own = gram[rows, :]
        high = second_coef * own + third_coef * product(own, gram_head, gram_tail)
        rest = first_coef * (low[rows, :] + high) + product(high, low_head, low_tail)
        head_ref[rows, :], tail_ref[rows, :] = split(rest * factor)


def polynomial(packed, width, scale):
    square = (width, width)

    def kernel(*refs):
        polynomial_kernel(scale, *refs)

    whole = pl.BlockSpec(memory_space=pltpu.VMEM)
    return pl.pallas_call(
        kernel,
        in_specs=[whole],
        out_specs=[whole] * 3,
        out_shape=[
            jax.ShapeDtypeStruct(square, jnp.bfloat16),
            jax.ShapeDtypeStruct(square, jnp.bfloat16),
            jax.ShapeDtypeStruct((8, width), jnp.float32),
        ],
        scratch_shapes=[
            pltpu.VMEM(square, jnp.float32),
            pltpu.VMEM(square, jnp.bfloat16),
            pltpu.VMEM(square, jnp.bfloat16),
        ]
        * 2,
        compiler_params=pltpu.CompilerParams(vmem_limit_bytes=40 * 2**20),
        cost_estimate=pl.CostEstimate(
            flops=30 * width**3, bytes_accessed=8 * width**2, transcendentals=0
        ),
    )(packed)


def apply_kernel(current_ref, head_ref, tail_ref, factor_ref, out_ref):
    values = current_ref[...]
    out_ref[...] = factor_ref[0:1, :] * values + product(values, head_ref, tail_ref)


def apply_polynomial(current, head, tail, factor):
    rows, width = current.shape
    tile = math.gcd(rows, 256)
    block = pl.BlockSpec((tile, width), lambda t: (t, 0))
    square = pl.BlockSpec((width, width), lambda t: (0, 0))
    return pl.pallas_call(
        apply_kernel,
        grid=(rows // tile,),
        in_specs=[block, square, square, pl.BlockSpec((8, width), lambda t: (0, 0))],
        out_specs=block,
        out_shape=jax.ShapeDtypeStruct((rows, width), jnp.float32),
        compiler_params=pltpu.CompilerParams(vmem_limit_bytes=32 * 2**20),
        cost_estimate=pl.CostEstimate(
            flops=6 * rows * width**2, bytes_accessed=8 * rows * width, transcendentals=0
        ),
    )(current, head, tail, factor)


def shards(grads, momentum, owner_table):
    mats = grads.shape[0]
    groups = lax.axis_size("far") * lax.axis_size("near")
    blocks = lax.axis_size("row")
    near = ("near", "row")
    in_window = owner_table < groups
    flags = in_window[:, None, None, None]
    group_ids = jnp.arange(groups, dtype=jnp.int32)
    matches = (owner_table[None, :] == group_ids[:, None]).astype(jnp.int32)
    chosen = jnp.sum(matches * jnp.arange(mats, dtype=jnp.int32)[None, :], axis=1)
    outgoing = pick_nesterov(chosen, grads, momentum, groups)
    rows, width = outgoing.shape[1:]
    owned = lax.all_to_all(outgoing, near, split_axis=0, concat_axis=0, tiled=True)
    new_momentum = jnp.where(flags, momentum_decay * momentum + grads, momentum)
    current = owned.reshape(groups * rows, width)
    scale = 0.2 * math.sqrt(max(rows * groups * blocks, width))
    packed = lax.psum(triangle(upper_gram(current)), "far")
    head, tail, factor = polynomial(packed, width, scale)
    result = apply_polynomial(current, head, tail, factor)
    returned = lax.all_to_all(
        result.reshape(groups, rows, width), near, split_axis=0, concat_axis=0, tiled=True
    )
    update = place_update(owner_table, returned, mats)
    return (new_momentum, update)


def solution(mesh):
    groups, blocks = mesh.shape["grp"], mesh.shape["row"]
    near = max(1, groups // blocks)
    assert near * blocks == groups
    split = Mesh(mesh.devices.reshape(groups // near, near, blocks), ("far", "near", "row"))
    spec = P(None, "row", ("far", "near"), None)
    return jax.shard_map(
        shards, mesh=split, in_specs=(spec, spec, P()), out_specs=(spec, spec), check_vma=False
    )
```

profile of v0, /device:TPU:0, one launch (start us, length us, event | category | flops | bytes accessed | tf_op | source)
XLA Modules:
  0.0 379.5 jit_solution(5139804317616476891)
XLA Ops:
  7.2 0.0 all-reduce.2.cloned.1.call-start
  7.2 1.3 select_reduce_fusion.chosen_ref
  8.5 10.8 %shard_map.50 = f32[8,224,1024]{2,1,0:T(8,128)} custom-call(s32[8]{0:T(128)} %select_reduce_fusion.chosen_ref, f32[12,1,224,1024]{3,2,1,0:T(8,128)} %grads_ref.1, f32[12,1,224,1024]{3,2,1,0:T(8,128)} %momentum_ref.1), custom_call_target="tpu_custom_call" | custom-call | flops 7340032 | bytes 22020096 | tf_op jit(solution)/shard_map/pallas_call | solution.py:34
  19.3 87.9 %all_to_all.10 = f32[8,224,1024]{2,1,0:T(8,128)S(1)} all-to-all(f32[8,224,1024]{2,1,0:T(8,128)} %shard_map.50), channel_id=1, replica_groups=mesh['far'=4,'near'=2,'row'=4] {'near','row'}, dimensions={0} | all-to-all | bytes 14680064 | tf_op jit(solution)/shard_map/all_to_all | solution.py:251
  107.3 1.7 fusion.4
  109.0 1.8 fusion.2
  110.7 3.0 fusion
  113.8 0.0 copy-done
  113.8 3.6 fusion.8
  117.7 0.0 copy-start.4
  117.7 1.4 copy-done.4
  119.1 0.0 all-reduce.2.cloned.1.call-update
  119.1 95.2 %all-reduce.2.cloned.1.call-done.refs_0_ = f32[128,4608]{1,0:T(8,128)} async-done(((f32[128,4608]{1,0:T(8,128)}), f32[128,4608]{1,0:T(8,128)}) %all-reduce.2.cloned.1.call-update) | async-done | bytes 2359312 | tf_op jit(solution)/shard_map/psum | solution.py:255
  214.3 1.7 copy-done.3
  215.9 37.2 %shard_map.51 = (bf16[1024,1024]{1,0:T(8,128)(2,1)S(1)}, bf16[1024,1024]{1,0:T(8,128)(2,1)S(1)}, f32[8,1024]{1,0:T(8,128)S(1)}) custom-call(f32[128,4608]{1,0:T(8,128)S(1)} %copy-done.3), custom_call_target="tpu_custom_call" | custom-call | flops 32212254720 | bytes 8388608 | tf_op jit(solution)/shard_map/pallas_call | solution.py:194
  253.1 0.0 copy-start.1
  253.1 3.1 copy-done.1
  256.2 12.6 %shard_map.52 = f32[1792,1024]{1,0:T(8,128)S(1)} custom-call(f32[1792,1024]{1,0:T(8,128)S(1)} %bitcast.7, bf16[1024,1024]{1,0:T(8,128)(2,1)S(1)} %get-tuple-element.5.head_ref, bf16[1024,1024]{1,0:T(8,128)(2,1)S(1)} %get-tuple-element.6.tail_ref, f32[8,1024]{1,0:T(8,128)S(1)} %get-tuple-element.7.factor_ref), custom_call_target="tpu_custom_call" | custom-call | flops 11274289152 | bytes 14680064 | tf_op jit(solution)/shard_map/pallas_call | solution.py:226
  268.8 0.0 copy-start.2
  268.8 3.0 copy-done.2
  271.8 5.0 %all-to-all-start.1 = ((f32[8,224,1024]{2,1,0:T(8,128)}), f32[8,224,1024]{2,1,0:T(8,128)}, u32[]{:S(2)}, u32[]{:S(2)}) async-start(f32[8,224,1024]{2,1,0:T(8,128)} %bitcast.8), calls=%async_computation.1 | async-start | bytes 14680064 | tf_op jit(solution)/shard_map/all_to_all | solution.py:258
  276.9 13.6 %add_select_fusion = f32[12,1,224,1024]{3,2,1,0:T(8,128)} fusion(f32[12,1,224,1024]{3,2,1,0:T(8,128)} %momentum_ref.1, f32[12,1,224,1024]{3,2,1,0:T(8,128)} %grads_ref.1, pred[12]{0:T(512)(128)(4,1)S(1)} %broadcast_compare_fusion), kind=kLoop, calls=%fused_computation | loop fusion | flops 8257536 | bytes 33030156 | tf_op jit(solution)/shard_map/jit(_where)/select_n | solution.py:252
  290.4 69.2 %all-to-all-done.1.refs_1_ = f32[8,224,1024]{2,1,0:T(8,128)} async-done(((f32[8,224,1024]{2,1,0:T(8,128)}), f32[8,224,1024]{2,1,0:T(8,128)}, u32[]{:S(2)}, u32[]{:S(2)}) %all-to-all-start.1) | async-done | bytes 7340064 | tf_op jit(solution)/shard_map/all_to_all | solution.py:258
  359.7 13.0 %shard_map.53 = f32[12,1,224,1024]{3,2,1,0:T(8,128)} custom-call(s32[12]{0:T(128)} %refs_0_.1, f32[8,224,1024]{2,1,0:T(8,128)} %all-to-all-done.1.refs_1_), custom_call_target="tpu_custom_call" | custom-call | bytes 18350080 | tf_op jit(solution)/shard_map/pallas_call | solution.py:67
  (13 shorter events, 0.2 us)
Async XLA Ops:
  7.2 207.1 %all-reduce.2.cloned.1.call-start = ((), (), s32[]{:S(2)}) async-start(), calls=%async_computation.2 | async-start | bytes 4718592 | tf_op jit(solution)/shard_map/psum | solution.py:255
  107.3 6.5 %copy-start = (f32[8,224,1024]{2,1,0:T(8,128)}, f32[8,224,1024]{2,1,0:T(8,128)S(1)}, u32[]{:S(2)}) copy-start(f32[8,224,1024]{2,1,0:T(8,128)S(1)} %all_to_all.10) | copy-start | bytes 22020100
  117.7 1.4 copy-start.4
  214.3 1.7 copy-start.3
  253.1 3.1 copy-start.1
  268.8 3.1 copy-start.2
  271.8 5.0 %copy-start.5 = (s32[12]{0:T(128)S(1)}, s32[12]{0:T(128)}, u32[]{:S(2)}) copy-start(s32[12]{0:T(128)} %refs_0_.1) | copy-start | bytes 148
  271.8 87.8 %all-to-all-start.1 = ((f32[8,224,1024]{2,1,0:T(8,128)}), f32[8,224,1024]{2,1,0:T(8,128)}, u32[]{:S(2)}, u32[]{:S(2)}) async-start(f32[8,224,1024]{2,1,0:T(8,128)} %bitcast.8), calls=%async_computation.1 | async-start | bytes 14680064 | tf_op jit(solution)/shard_map/all_to_all | solution.py:258
Sparse Core Ops, SparseCore 0:
  119.2 95.0 all-reduce.1
where the time goes:
time: 380 us; the launch traced here: 379 us
  waiting for transfers between devices  164 us (43%)
  blocking collectives  87.9 us (23%)
  Pallas kernels  73.6 us (19%)
  other arithmetic  14.9 us (4%)
  between operations  14.2 us (4%)
  matrix products  10.1 us (3%)
  local copies, waits for them, and re-layouts  9.39 us (2%)
  starting transfers between devices  5.04 us (1%)
    psum x1, waiting for transfers between devices, shards(): packed = lax.psum(triangle(upper_gram(current)), 'far')  95.2 us
    all_to_all x1, blocking collectives, shards(): lax.all_to_all(outgoing, near, split_axis=0, concat_axis=0, tiled=True)  87.9 us
    all_to_all x1, waiting for transfers between devices, shards(): lax.all_to_all(result.reshape(groups, rows, width), near, split_axis=0, c...  69.2 us
    pallas_call x1, Pallas kernels, polynomial(): pl.pallas_call(kernel, in_specs=[whole], out_specs=[whole] * 3, out_shape...  37.2 us
    select_n x1, other arithmetic, shards(): new_momentum = jnp.where(flags, momentum_decay * momentum + grads, momentum)  13.6 us
    pallas_call x1, Pallas kernels, place_update(): pl.pallas_call(kernel, grid_spec=pltpu.PrefetchScalarGridSpec(num_scalar_...  13 us
    pallas_call x1, Pallas kernels, apply_polynomial(): pl.pallas_call(apply_kernel, grid=(rows // tile,), in_specs=[block, squar...  12.6 us
    pallas_call x1, Pallas kernels, pick_nesterov(): pl.pallas_call(pick_kernel, grid_spec=pltpu.PrefetchScalarGridSpec(num_sc...  10.8 us
  transfers between devices with their start and end apart: 2, of which 2 were waited for; matrix products, arithmetic and copies ran while one was open for 4% of the time, Pallas kernels for 0%

commit v1 on v0

--- a/solution.py
+++ b/solution.py
@@ -46,37 +46,40 @@
     )(chosen, grads, momentum)
 
 
-def place_kernel(groups, owner_ref, returned_ref, out_ref):
-    inside = owner_ref[pl.program_id(0)] < groups
-
-    @pl.when(inside)
-    def _():
-        out_ref[0, 0] = returned_ref[0]
-
-    @pl.when(jnp.logical_not(inside))
-    def _():
-        out_ref[...] = jnp.zeros_like(out_ref)
+def place_kernel(owner_ref, returned_ref, out_ref, zeros, sems):
+    groups, mats = returned_ref.shape[0], out_ref.shape[0]
+    zeros[...] = jnp.zeros_like(zeros)
+    for k in range(mats):
+        owner = owner_ref[k]
+        slot = jnp.minimum(owner, groups - 1)
+
+        @pl.when(owner < groups)
+        def _(k=k, slot=slot):
+            pltpu.make_async_copy(returned_ref.at[slot], out_ref.at[k, 0], sems.at[k]).start()
+
+        @pl.when(owner >= groups)
+        def _(k=k):
+            pltpu.make_async_copy(zeros, out_ref.at[k, 0], sems.at[k]).start()
+
+    for k in range(mats):
+        pltpu.make_async_copy(zeros, out_ref.at[k, 0], sems.at[k]).wait()
 
 
 def place_update(owner_table, returned, mats):
     groups, rows, width = returned.shape
-
-    def kernel(*refs):
-        place_kernel(groups, *refs)
-
-    return pl.pallas_call(
-        kernel,
-        grid_spec=pltpu.PrefetchScalarGridSpec(
-            num_scalar_prefetch=1,
-            grid=(mats,),
-            in_specs=[
-                pl.BlockSpec(
-                    (1, rows, width), lambda k, owner: (jnp.minimum(owner[k], groups - 1), 0, 0)
-                )
-            ],
-            out_specs=pl.BlockSpec((1, 1, rows, width), lambda k, owner: (k, 0, 0, 0)),
-        ),
+    return pl.pallas_call(
+        place_kernel,
+        in_specs=[
+            pl.BlockSpec(memory_space=pltpu.SMEM),
+            pl.BlockSpec(memory_space=pltpu.VMEM),
+        ],
+        out_specs=pl.BlockSpec(memory_space=pl.ANY),
         out_shape=jax.ShapeDtypeStruct((mats, 1, rows, width), jnp.float32),
+        scratch_shapes=[
+            pltpu.VMEM((rows, width), jnp.float32),
+            pltpu.SemaphoreType.DMA((mats,)),
+        ],
+        compiler_params=pltpu.CompilerParams(vmem_limit_bytes=32 * 2**20),
         cost_estimate=pl.CostEstimate(
             flops=0, bytes_accessed=4 * (groups + mats) * rows * width, transcendentals=0
         ),

time: 380 us -> 374 us (0.984)
  Pallas kernels: 73.6 us -> 67.9 us
    pallas_call x1, Pallas kernels: 13 us -> 7.34 us  [place_update(): pl.pallas_call(place_kernel, in_specs=[pl.BlockSpec(memory_space=pltpu.SM...]
where the time goes in v1:
time: 374 us
  waiting for transfers between devices  164 us (44%)
  blocking collectives  87.9 us (24%)
  Pallas kernels  67.9 us (18%)
  other arithmetic  14.9 us (4%)
  between operations  14.2 us (4%)
  matrix products  10.1 us (3%)
  local copies, waits for them, and re-layouts  9.39 us (3%)
  starting transfers between devices  5.04 us (1%)
    psum x1, waiting for transfers between devices, shards(): packed = lax.psum(triangle(upper_gram(current)), 'far')  95.2 us
    all_to_all x1, blocking collectives, shards(): lax.all_to_all(outgoing, near, split_axis=0, concat_axis=0, tiled=True)  87.9 us
    all_to_all x1, waiting for transfers between devices, shards(): lax.all_to_all(result.reshape(groups, rows, width), near, split_axis=0, c...  69.2 us
    pallas_call x1, Pallas kernels, polynomial(): pl.pallas_call(kernel, in_specs=[whole], out_specs=[whole] * 3, out_shape...  37.2 us
    select_n x1, other arithmetic, shards(): new_momentum = jnp.where(flags, momentum_decay * momentum + grads, momentum)  13.6 us
    pallas_call x1, Pallas kernels, apply_polynomial(): pl.pallas_call(apply_kernel, grid=(rows // tile,), in_specs=[block, squar...  12.6 us
    pallas_call x1, Pallas kernels, pick_nesterov(): pl.pallas_call(pick_kernel, grid_spec=pltpu.PrefetchScalarGridSpec(num_sc...  10.8 us
    dot_general x4, matrix products, dot3(): lax.dot_general(left, right, dims, precision=lax.Precision.HIGH, preferre...  10.1 us
  transfers between devices with their start and end apart: 2, of which 2 were waited for; matrix products, arithmetic and copies ran while one was open for 4% of the time, Pallas kernels for 0%

profile of v1, /device:TPU:0, one launch (start us, length us, event | category | flops | bytes accessed | tf_op | source)
XLA Modules:
  0.0 373.9 jit_solution(1657596826128105764)
XLA Ops:
  7.2 0.0 all-reduce.2.cloned.1.call-start
  7.2 1.3 select_reduce_fusion.chosen_ref
  8.5 10.8 %shard_map.50 = f32[8,224,1024]{2,1,0:T(8,128)} custom-call(s32[8]{0:T(128)} %select_reduce_fusion.chosen_ref, f32[12,1,224,1024]{3,2,1,0:T(8,128)} %grads_ref.1, f32[12,1,224,1024]{3,2,1,0:T(8,128)} %momentum_ref.1), custom_call_target="tpu_custom_call" | custom-call | flops 7340032 | bytes 22020096 | tf_op jit(solution)/shard_map/pallas_call | solution.py:34
  19.3 87.9 %all_to_all.10 = f32[8,224,1024]{2,1,0:T(8,128)S(1)} all-to-all(f32[8,224,1024]{2,1,0:T(8,128)} %shard_map.50), channel_id=1, replica_groups=mesh['far'=4,'near'=2,'row'=4] {'near','row'}, dimensions={0} | all-to-all | bytes 14680064 | tf_op jit(solution)/shard_map/all_to_all | solution.py:254
  107.3 1.7 fusion.4
  109.0 1.8 fusion.2
  110.7 3.0 fusion
  113.8 0.0 copy-done
  113.8 3.6 fusion.8
  117.7 0.0 copy-start.5
  117.7 1.4 copy-done.5
  119.1 0.0 all-reduce.2.cloned.1.call-update
  119.1 95.2 %all-reduce.2.cloned.1.call-done.refs_0_ = f32[128,4608]{1,0:T(8,128)} async-done(((f32[128,4608]{1,0:T(8,128)}), f32[128,4608]{1,0:T(8,128)}) %all-reduce.2.cloned.1.call-update) | async-done | bytes 2359312 | tf_op jit(solution)/shard_map/psum | solution.py:258
  214.3 1.7 copy-done.4
  215.9 37.2 %shard_map.51 = (bf16[1024,1024]{1,0:T(8,128)(2,1)S(1)}, bf16[1024,1024]{1,0:T(8,128)(2,1)S(1)}, f32[8,1024]{1,0:T(8,128)S(1)}) custom-call(f32[128,4608]{1,0:T(8,128)S(1)} %copy-done.4), custom_call_target="tpu_custom_call" | custom-call | flops 32212254720 | bytes 8388608 | tf_op jit(solution)/shard_map/pallas_call | solution.py:197
  253.1 0.0 copy-start.1
  253.1 3.1 copy-done.1
  256.2 12.6 %shard_map.52 = f32[1792,1024]{1,0:T(8,128)S(1)} custom-call(f32[1792,1024]{1,0:T(8,128)S(1)} %bitcast.7, bf16[1024,1024]{1,0:T(8,128)(2,1)S(1)} %get-tuple-element.5.head_ref, bf16[1024,1024]{1,0:T(8,128)(2,1)S(1)} %get-tuple-element.6.tail_ref, f32[8,1024]{1,0:T(8,128)S(1)} %get-tuple-element.7.factor_ref), custom_call_target="tpu_custom_call" | custom-call | flops 11274289152 | bytes 14680064 | tf_op jit(solution)/shard_map/pallas_call | solution.py:229
  268.8 0.0 copy-start.2
  268.8 3.0 copy-done.2
  271.8 5.0 %all-to-all-start.1 = ((f32[8,224,1024]{2,1,0:T(8,128)}), f32[8,224,1024]{2,1,0:T(8,128)}, u32[]{:S(2)}, u32[]{:S(2)}) async-start(f32[8,224,1024]{2,1,0:T(8,128)} %bitcast.8), calls=%async_computation.1 | async-start | bytes 14680064 | tf_op jit(solution)/shard_map/all_to_all | solution.py:261
  276.9 13.6 %add_select_fusion = f32[12,1,224,1024]{3,2,1,0:T(8,128)} fusion(f32[12,1,224,1024]{3,2,1,0:T(8,128)} %momentum_ref.1, f32[12,1,224,1024]{3,2,1,0:T(8,128)} %grads_ref.1, pred[12]{0:T(512)(128)(4,1)S(1)} %broadcast_compare_fusion), kind=kLoop, calls=%fused_computation | loop fusion | flops 8257536 | bytes 33030156 | tf_op jit(solution)/shard_map/jit(_where)/select_n | solution.py:255
  290.4 69.2 %all-to-all-done.1.returned_ref = f32[8,224,1024]{2,1,0:T(8,128)} async-done(((f32[8,224,1024]{2,1,0:T(8,128)}), f32[8,224,1024]{2,1,0:T(8,128)}, u32[]{:S(2)}, u32[]{:S(2)}) %all-to-all-start.1) | async-done | bytes 7340064 | tf_op jit(solution)/shard_map/all_to_all | solution.py:261
  359.7 7.3 %shard_map.53 = f32[12,1,224,1024]{3,2,1,0:T(8,128)} custom-call(s32[12]{0:T(128)S(1)} %copy-done.3, f32[8,224,1024]{2,1,0:T(8,128)} %all-to-all-done.1.returned_ref), custom_call_target="tpu_custom_call" | custom-call | bytes 18350080 | tf_op jit(solution)/shard_map/pallas_call | solution.py:70
  (13 shorter events, 0.2 us)
Async XLA Ops:
  7.2 207.1 %all-reduce.2.cloned.1.call-start = ((), (), s32[]{:S(2)}) async-start(), calls=%async_computation.2 | async-start | bytes 4718592 | tf_op jit(solution)/shard_map/psum | solution.py:258
  107.3 6.5 %copy-start = (f32[8,224,1024]{2,1,0:T(8,128)}, f32[8,224,1024]{2,1,0:T(8,128)S(1)}, u32[]{:S(2)}) copy-start(f32[8,224,1024]{2,1,0:T(8,128)S(1)} %all_to_all.10) | copy-start | bytes 22020100
  117.7 1.4 copy-start.5
  214.3 1.7 copy-start.4
  253.1 3.1 copy-start.1
  268.8 3.1 copy-start.2
  271.8 5.0 %copy-start.3 = (s32[12]{0:T(128)S(1)}, s32[12]{0:T(128)}, u32[]{:S(2)}) copy-start(s32[12]{0:T(128)} %owner_ref.1) | copy-start | bytes 148
  271.8 87.8 %all-to-all-start.1 = ((f32[8,224,1024]{2,1,0:T(8,128)}), f32[8,224,1024]{2,1,0:T(8,128)}, u32[]{:S(2)}, u32[]{:S(2)}) async-start(f32[8,224,1024]{2,1,0:T(8,128)} %bitcast.8), calls=%async_computation.1 | async-start | bytes 14680064 | tf_op jit(solution)/shard_map/all_to_all | solution.py:261
Sparse Core Ops, SparseCore 0:
  119.2 95.0 all-reduce.1
